TPU v7x, 512 devices: a whole 4x4x16 slice. The times are simulated.
512 devices in a mesh: blk: 32 (over y_hi, z), row: 16 (over x, y_lo, core).
Axes of the slice: x: 4, y: 4 (y_hi: 2, y_lo: 2; y = y_hi * 2 + y_lo), z: 16, core: 2. Of those that a mesh axis runs over, the one named last changes fastest.
Arguments:
- features: bfloat16 [65536, 128], P(('blk', 'row')), may hold values from -6 to 6
- targets: float32 [65536, 64], P(('blk', 'row')), may hold values from -6 to 6
- round_masks: int32 [2], replicated, may hold values from 1 to 31, as said below
Outputs:
- solution: float32 [65536, 64], P(('blk', 'row'))
- residual: float32 [65536, 64], P(('blk', 'row'))
Inputs may be any that keep to these rules, and one draw needn't show every extreme that they name: `round_masks`: 2 distinct numbers, one of which is always 32 - 1.
All inputs are finite; a program needn't handle non-finite values.
Results may differ from a plain program's by a relative error of at most 0.0024.
The roundings to bfloat16 on the way count: a program that leaves them out, or rounds other values in their place, can miss the bound.
Values may be sent and summed in bfloat16 or wider, within the bound.
A program may use at most 64 MiB of HBM per device.

v0:
```python
import jax
import jax.numpy as jnp
from jax import lax
from jax.sharding import PartitionSpec as P

ROUNDS = 2
ITERS = 3


RIDGE = 1.0


def from_partner(block, axis, stride):
    count = lax.axis_size(axis)
    route = []
    for low in range(count):
        high = low | 1 << stride
        if high != low and high < count:
            route += [(low, high), (high, low)]
    return lax.ppermute(block, axis, route)


def kernel_tile(left, left_sq, right, right_sq):
    inner_products = lax.dot_general(
        left, right, (((1,), (1,)), ((), ())), preferred_element_type=jnp.float32
    )
    feature_width = left.shape[1]
    exponent = (2.0 * inner_products - left_sq[:, None] - right_sq[None, :]) / feature_width
    return jnp.exp(exponent).astype(jnp.bfloat16)


def row_squares(values):
    return jnp.sum(jnp.square(values.astype(jnp.float32)), axis=1)


def local(features, targets, round_masks):
    hop_count = lax.axis_size("blk").bit_length() - 1
    local_rows = features.shape[0]
    own_sq = row_squares(features)
    block_features = lax.all_gather(features, "row", axis=0, tiled=True)
    block_sq = row_squares(block_features)

    def bit_chosen(round_index, bit_index):
        return jnp.bitwise_and(jnp.right_shift(round_masks[round_index], bit_index), 1) == 1

    results = []
    for round_index in range(ROUNDS):
        fetched = features
        for bit_index in range(hop_count):
            swapped = from_partner(fetched, "blk", bit_index)
            fetched = jnp.where(bit_chosen(round_index, bit_index), swapped, fetched)
        results.append(fetched)
    partner_blocks = [lax.all_gather(group, "row", axis=0, tiled=True) for group in results]
    own_tile = kernel_tile(features, own_sq, block_features, block_sq)
    partner_tiles = [
        kernel_tile(features, own_sq, block, row_squares(block)) for block in partner_blocks
    ]

    def fold_against(tile):

        def folder(accumulated, portion, offset):
            return jnp.dot(tile, portion, preferred_element_type=jnp.float32)

        return folder

    def total_squares(values):
        return lax.psum(jnp.sum(values * values, axis=0), ("blk", "row"))

    solution = jnp.zeros(targets.shape, jnp.float32)
    residual = targets
    direction = targets
    norm_now = total_squares(residual)
    for iteration in range(ITERS):
        apply_rounded = direction.astype(jnp.bfloat16)
        zero_sum = jnp.zeros((local_rows, apply_rounded.shape[1]), jnp.float32)
        own_part = fold_against(own_tile)(
            zero_sum, lax.all_gather(apply_rounded, "row", axis=0, tiled=True), jnp.int32(0)
        )
        products = ROUNDS * own_part
        fetch_results = []
        for fetch_round_index in range(ROUNDS):
            fetch_fetched = apply_rounded
            for fetch_bit_index in range(hop_count):
                fetch_swapped = from_partner(fetch_fetched, "blk", fetch_bit_index)
                fetch_fetched = jnp.where(
                    bit_chosen(fetch_round_index, fetch_bit_index), fetch_swapped, fetch_fetched
                )
            fetch_results.append(fetch_fetched)
        for apply_round_index in range(ROUNDS):
            apply_folder = fold_against(partner_tiles[apply_round_index])
            products = products + apply_folder(
                zero_sum,
                lax.all_gather(fetch_results[apply_round_index], "row", axis=0, tiled=True),
                jnp.int32(0),
            )
        applied = RIDGE * direction + products
        curvature = lax.psum(jnp.sum(direction * applied, axis=0), ("blk", "row"))
        step_size = norm_now / curvature
        solution = solution + step_size * direction
        residual = residual - step_size * applied
        norm_next = total_squares(residual)
        direction = residual + norm_next / norm_now * direction
        norm_now = norm_next
    return (solution, residual)


def solution(mesh):
    in_specs = (P(("blk", "row"), None), P(("blk", "row"), None), P())
    out_specs = (P(("blk", "row"), None), P(("blk", "row"), None))
    return jax.shard_map(local, mesh=mesh, in_specs=in_specs, out_specs=out_specs, check_vma=False)
```

profile of v0, /device:TPU:1, one launch (start us, length us, event | category | flops | bytes accessed | tf_op | source)
XLA Modules:
  0.0 919.8 jit_solution(12327498193527374107)
XLA Ops:
  7.8 23.8 %all_gather.36 = bf16[2048,128]{1,0:T(8,128)(2,1)S(1)} all-gather(bf16[128,128]{1,0:T(8,128)(2,1)S(1)} %copy-done.1), channel_id=1, replica_groups=mesh['blk'=32,'row'=16] {'row'}, dimensions={0}, use_global_device_ids=true | all-gather | bytes 557056 | tf_op jit(solution)/shard_map/all_gather | solution.py:40
  31.6 18.7 %all_gather.37 = bf16[2048,64]{0,1:T(8,128)(2,1)S(1)} all-gather(bf16[128,64]{0,1:T(8,128)(2,1)S(1)} %convert_element_type.33), channel_id=1, replica_groups=mesh['blk'=32,'row'=16] {'row'}, dimensions={0}, use_global_device_ids=true | all-gather | bytes 278528 | tf_op jit(solution)/shard_map/all_gather | solution.py:77
  67.0 8.3 collective-permute-start.7
  80.5 11.9 %collective-permute-start.8 = (bf16[128,64]{0,1:T(8,128)(2,1)S(1)}, bf16[128,64]{0,1:T(8,128)(2,1)S(1)}, u32[]{:S(2)}, u32[]{:S(2)}) collective-permute-start(bf16[128,64]{0,1:T(8,128)(2,1)S(1)} %broadcast_select_fusion.33), channel_id=1, source_target_pairs={{0,128},{128,0},{16,144},{144,16},{32,160},{160,32},{48,176},{176,... | collective-permute-start | bytes 49160 | tf_op jit(solution)/shard_map/ppermute | solution.py:20
  111.8 22.4 %all_gather.39 = bf16[2048,64]{0,1:T(8,128)(2,1)S(1)} all-gather(bf16[128,64]{0,1:T(8,128)(2,1)S(1)} %broadcast_select_fusion.39), channel_id=1, replica_groups=mesh['blk'=32,'row'=16] {'row'}, dimensions={0}, use_global_device_ids=true | all-gather | bytes 278528 | tf_op jit(solution)/shard_map/all_gather | solution.py:93
  134.2 17.0 %all_gather.41 = bf16[2048,64]{0,1:T(8,128)(2,1)S(1)} all-gather(bf16[128,64]{0,1:T(8,128)(2,1)S(1)} %broadcast_select_fusion.24), channel_id=1, replica_groups=mesh['blk'=32,'row'=16] {'row'}, dimensions={0}, use_global_device_ids=true | all-gather | bytes 278528 | tf_op jit(solution)/shard_map/all_gather | solution.py:93
  151.2 10.3 %collective-permute-start.3 = (bf16[128,128]{1,0:T(8,128)(2,1)S(1)}, bf16[128,128]{1,0:T(8,128)(2,1)S(1)}, u32[]{:S(2)}, u32[]{:S(2)}) collective-permute-start(bf16[128,128]{1,0:T(8,128)(2,1)S(1)} %broadcast_select_fusion.7), channel_id=1, source_target_pairs={{0,128},{128,0},{16,144},{144,16},{32,160},{160,32},{48,176},{176,... | collective-permute-start | bytes 98312 | tf_op jit(solution)/shard_map/ppermute | solution.py:20
  169.8 7.4 collective-permute-done.12
  181.7 19.2 %all_gather.38 = bf16[2048,128]{1,0:T(8,128)(2,1)S(1)} all-gather(bf16[128,128]{1,0:T(8,128)(2,1)S(1)} %broadcast_select_fusion.9), channel_id=1, replica_groups=mesh['blk'=32,'row'=16] {'row'}, dimensions={0}, use_global_device_ids=true | all-gather | bytes 557056 | tf_op jit(solution)/shard_map/all_gather | solution.py:53
  201.8 18.3 %all_gather.40 = bf16[2048,128]{1,0:T(8,128)(2,1)S(1)} all-gather(bf16[128,128]{1,0:T(8,128)(2,1)S(1)} %broadcast_select_fusion.4), channel_id=1, replica_groups=mesh['blk'=32,'row'=16] {'row'}, dimensions={0}, use_global_device_ids=true | all-gather | bytes 557056 | tf_op jit(solution)/shard_map/all_gather | solution.py:53
  221.4 98.8 %all-reduce = (f32[64]{0:T(128)S(1)}, f32[64]{0:T(128)S(1)}) all-reduce(f32[64]{0:T(128)S(1)} %get-tuple-element.3, f32[64]{0:T(128)S(1)} %get-tuple-element.2), channel_id=1, replica_groups=mesh['blk'=32,'row'=16] {'blk','row'}, use_global_device_ids=true, to_apply=%region_1.0 | all-reduce | flops 128 | bytes 1024 | tf_op jit(solution)/shard_map/psum | solution.py:67
  320.4 100.1 %psum.44 = f32[64]{0:T(128)S(1)} all-reduce(f32[64]{0:T(128)S(1)} %multiply_reduce_fusion.7), channel_id=1, replica_groups=mesh['blk'=32,'row'=16] {'blk','row'}, use_global_device_ids=true, to_apply=%region_9.10 | all-reduce | flops 64 | bytes 512 | tf_op jit(solution)/shard_map/psum | solution.py:67
  423.4 18.9 %all_gather.42 = bf16[2048,64]{0,1:T(8,128)(2,1)S(1)} all-gather(bf16[128,64]{0,1:T(8,128)(2,1)S(1)} %get-tuple-element.10), channel_id=1, replica_groups=mesh['blk'=32,'row'=16] {'row'}, dimensions={0}, use_global_device_ids=true | all-gather | bytes 278528 | tf_op jit(solution)/shard_map/all_gather | solution.py:77
  458.1 6.3 collective-permute-start.21
  464.4 7.7 collective-permute-start.25
  481.6 19.4 %all_gather.43 = bf16[2048,64]{0,1:T(8,128)(2,1)S(1)} all-gather(bf16[128,64]{0,1:T(8,128)(2,1)S(1)} %broadcast_select_fusion.38), channel_id=1, replica_groups=mesh['blk'=32,'row'=16] {'row'}, dimensions={0}, use_global_device_ids=true | all-gather | bytes 278528 | tf_op jit(solution)/shard_map/all_gather | solution.py:93
  501.0 18.6 %all_gather.44 = bf16[2048,64]{0,1:T(8,128)(2,1)S(1)} all-gather(bf16[128,64]{0,1:T(8,128)(2,1)S(1)} %broadcast_select_fusion.23), channel_id=1, replica_groups=mesh['blk'=32,'row'=16] {'row'}, dimensions={0}, use_global_device_ids=true | all-gather | bytes 278528 | tf_op jit(solution)/shard_map/all_gather | solution.py:93
  520.2 98.8 %psum.45 = f32[64]{0:T(128)S(1)} all-reduce(f32[64]{0:T(128)S(1)} %get-tuple-element.25), channel_id=1, replica_groups=mesh['blk'=32,'row'=16] {'blk','row'}, use_global_device_ids=true, to_apply=%region_11.12 | all-reduce | flops 64 | bytes 512 | tf_op jit(solution)/shard_map/psum | solution.py:97
  619.2 99.6 %psum.46 = f32[64]{0:T(128)S(1)} all-reduce(f32[64]{0:T(128)S(1)} %get-tuple-element.8), channel_id=1, replica_groups=mesh['blk'=32,'row'=16] {'blk','row'}, use_global_device_ids=true, to_apply=%region_13.14 | all-reduce | flops 64 | bytes 512 | tf_op jit(solution)/shard_map/psum | solution.py:67
  721.6 18.9 %all_gather.45 = bf16[2048,64]{0,1:T(8,128)(2,1)S(1)} all-gather(bf16[128,64]{0,1:T(8,128)(2,1)S(1)} %get-tuple-element.6), channel_id=1, replica_groups=mesh['blk'=32,'row'=16] {'row'}, dimensions={0}, use_global_device_ids=true | all-gather | bytes 278528 | tf_op jit(solution)/shard_map/all_gather | solution.py:77
  756.3 8.0 collective-permute-start.30
  781.6 19.6 %all_gather.46 = bf16[2048,64]{0,1:T(8,128)(2,1)S(1)} all-gather(bf16[128,64]{0,1:T(8,128)(2,1)S(1)} %broadcast_select_fusion.37), channel_id=1, replica_groups=mesh['blk'=32,'row'=16] {'row'}, dimensions={0}, use_global_device_ids=true | all-gather | bytes 278528 | tf_op jit(solution)/shard_map/all_gather | solution.py:93
  801.2 18.6 %all_gather.47 = bf16[2048,64]{0,1:T(8,128)(2,1)S(1)} all-gather(bf16[128,64]{0,1:T(8,128)(2,1)S(1)} %broadcast_select_fusion.22), channel_id=1, replica_groups=mesh['blk'=32,'row'=16] {'row'}, dimensions={0}, use_global_device_ids=true | all-gather | bytes 278528 | tf_op jit(solution)/shard_map/all_gather | solution.py:93
  820.4 98.7 %psum.47 = f32[64]{0:T(128)S(1)} all-reduce(f32[64]{0:T(128)S(1)} %get-tuple-element.27), channel_id=1, replica_groups=mesh['blk'=32,'row'=16] {'blk','row'}, use_global_device_ids=true, to_apply=%region_15.16 | all-reduce | flops 64 | bytes 512 | tf_op jit(solution)/shard_map/psum | solution.py:97
  (135 shorter events, 122.6 us)
Async XLA Ops:
  0.6 64.4 %collective-permute-start = (bf16[128,128]{1,0:T(8,128)(2,1)}, bf16[128,128]{1,0:T(8,128)(2,1)S(1)}, u32[]{:S(2)}, u32[]{:S(2)}) collective-permute-start(bf16[128,128]{1,0:T(8,128)(2,1)} %param.3), channel_id=1, source_target_pairs={{0,16},{16,0},{32,48},{48,32},{64,80},{80,64},{96,112},{112,96},{1... | collective-permute-start | bytes 98312 | tf_op jit(solution)/shard_map/ppermute | solution.py:20
  5.8 53.0 %collective-permute-start.5 = (bf16[128,64]{0,1:T(8,128)(2,1)S(1)}, bf16[128,64]{0,1:T(8,128)(2,1)S(1)}, u32[]{:S(2)}, u32[]{:S(2)}) collective-permute-start(bf16[128,64]{0,1:T(8,128)(2,1)S(1)} %convert_element_type.33), channel_id=1, source_target_pairs={{0,16},{16,0},{32,48},{48,32},{64,80},{80,64},{96,112},{112,96},{1... | collective-permute-start | bytes 49160 | tf_op jit(solution)/shard_map/ppermute | solution.py:20
  60.7 16.5 %collective-permute-start.14 = (bf16[128,64]{0,1:T(8,128)(2,1)S(1)}, bf16[128,64]{0,1:T(8,128)(2,1)S(1)}, u32[]{:S(2)}, u32[]{:S(2)}) collective-permute-start(bf16[128,64]{0,1:T(8,128)(2,1)S(1)} %get-tuple-element.19), channel_id=1, source_target_pairs={{0,32},{32,0},{16,48},{48,16},{64,96},{96,64},{80,112},{112,80},{1... | collective-permute-start | bytes 49160 | tf_op jit(solution)/shard_map/ppermute | solution.py:20
  65.0 30.6 %collective-permute-start.1 = (bf16[128,128]{1,0:T(8,128)(2,1)S(1)}, bf16[128,128]{1,0:T(8,128)(2,1)S(1)}, u32[]{:S(2)}, u32[]{:S(2)}) collective-permute-start(bf16[128,128]{1,0:T(8,128)(2,1)S(1)} %get-tuple-element.12), channel_id=1, source_target_pairs={{0,32},{32,0},{16,48},{48,16},{64,96},{96,64},{80,112},{112,80},{1... | collective-permute-start | bytes 98312 | tf_op jit(solution)/shard_map/ppermute | solution.py:20
  67.0 13.5 %collective-permute-start.7 = (bf16[128,64]{0,1:T(8,128)(2,1)S(1)}, bf16[128,64]{0,1:T(8,128)(2,1)S(1)}, u32[]{:S(2)}, u32[]{:S(2)}) collective-permute-start(bf16[128,64]{0,1:T(8,128)(2,1)S(1)} %broadcast_select_fusion.30), channel_id=1, source_target_pairs={{0,64},{64,0},{16,80},{80,16},{32,96},{96,32},{48,112},{112,48},{1... | collective-permute-start | bytes 49160 | tf_op jit(solution)/shard_map/ppermute | solution.py:20
  75.3 30.1 %collective-permute-start.10 = (bf16[128,128]{1,0:T(8,128)(2,1)S(1)}, bf16[128,128]{1,0:T(8,128)(2,1)S(1)}, u32[]{:S(2)}, u32[]{:S(2)}) collective-permute-start(bf16[128,128]{1,0:T(8,128)(2,1)S(1)} %get-tuple-element.13), channel_id=1, source_target_pairs={{0,32},{32,0},{16,48},{48,16},{64,96},{96,64},{80,112},{112,80},{1... | collective-permute-start | bytes 98312 | tf_op jit(solution)/shard_map/ppermute | solution.py:20
  77.2 15.2 %collective-permute-start.15 = (bf16[128,64]{0,1:T(8,128)(2,1)S(1)}, bf16[128,64]{0,1:T(8,128)(2,1)S(1)}, u32[]{:S(2)}, u32[]{:S(2)}) collective-permute-start(bf16[128,64]{0,1:T(8,128)(2,1)S(1)} %broadcast_select_fusion.15), channel_id=1, source_target_pairs={{0,64},{64,0},{16,80},{80,16},{32,96},{96,32},{48,112},{112,48},{1... | collective-permute-start | bytes 49160 | tf_op jit(solution)/shard_map/ppermute | solution.py:20
  80.5 20.3 %collective-permute-start.8 = (bf16[128,64]{0,1:T(8,128)(2,1)S(1)}, bf16[128,64]{0,1:T(8,128)(2,1)S(1)}, u32[]{:S(2)}, u32[]{:S(2)}) collective-permute-start(bf16[128,64]{0,1:T(8,128)(2,1)S(1)} %broadcast_select_fusion.33), channel_id=1, source_target_pairs={{0,128},{128,0},{16,144},{144,16},{32,160},{160,32},{48,176},{176,... | collective-permute-start | bytes 49160 | tf_op jit(solution)/shard_map/ppermute | solution.py:20
  92.5 17.0 %collective-permute-start.16 = (bf16[128,64]{0,1:T(8,128)(2,1)S(1)}, bf16[128,64]{0,1:T(8,128)(2,1)S(1)}, u32[]{:S(2)}, u32[]{:S(2)}) collective-permute-start(bf16[128,64]{0,1:T(8,128)(2,1)S(1)} %broadcast_select_fusion.18), channel_id=1, source_target_pairs={{0,128},{128,0},{16,144},{144,16},{32,160},{160,32},{48,176},{176,... | collective-permute-start | bytes 49160 | tf_op jit(solution)/shard_map/ppermute | solution.py:20
  95.7 55.5 %collective-permute-start.2 = (bf16[128,128]{1,0:T(8,128)(2,1)S(1)}, bf16[128,128]{1,0:T(8,128)(2,1)S(1)}, u32[]{:S(2)}, u32[]{:S(2)}) collective-permute-start(bf16[128,128]{1,0:T(8,128)(2,1)S(1)} %broadcast_select_fusion.6), channel_id=1, source_target_pairs={{0,64},{64,0},{16,80},{80,16},{32,96},{96,32},{48,112},{112,48},{1... | collective-permute-start | bytes 98312 | tf_op jit(solution)/shard_map/ppermute | solution.py:20
  105.4 56.0 %collective-permute-start.11 = (bf16[128,128]{1,0:T(8,128)(2,1)S(1)}, bf16[128,128]{1,0:T(8,128)(2,1)S(1)}, u32[]{:S(2)}, u32[]{:S(2)}) collective-permute-start(bf16[128,128]{1,0:T(8,128)(2,1)S(1)} %broadcast_select_fusion.1), channel_id=1, source_target_pairs={{0,64},{64,0},{16,80},{80,16},{32,96},{96,32},{48,112},{112,48},{1... | collective-permute-start | bytes 98312 | tf_op jit(solution)/shard_map/ppermute | solution.py:20
  109.5 24.7 %collective-permute-start.17 = (bf16[128,64]{0,1:T(8,128)(2,1)S(1)}, bf16[128,64]{0,1:T(8,128)(2,1)S(1)}, u32[]{:S(2)}, u32[]{:S(2)}) collective-permute-start(bf16[128,64]{0,1:T(8,128)(2,1)S(1)} %broadcast_select_fusion.21), channel_id=1, source_target_pairs={{0,256},{256,0},{16,272},{272,16},{32,288},{288,32},{48,304},{304,... | collective-permute-start | bytes 49160 | tf_op jit(solution)/shard_map/ppermute | solution.py:20
  151.2 14.0 %collective-permute-start.3 = (bf16[128,128]{1,0:T(8,128)(2,1)S(1)}, bf16[128,128]{1,0:T(8,128)(2,1)S(1)}, u32[]{:S(2)}, u32[]{:S(2)}) collective-permute-start(bf16[128,128]{1,0:T(8,128)(2,1)S(1)} %broadcast_select_fusion.7), channel_id=1, source_target_pairs={{0,128},{128,0},{16,144},{144,16},{32,160},{160,32},{48,176},{176,... | collective-permute-start | bytes 98312 | tf_op jit(solution)/shard_map/ppermute | solution.py:20
  161.5 15.7 %collective-permute-start.12 = (bf16[128,128]{1,0:T(8,128)(2,1)S(1)}, bf16[128,128]{1,0:T(8,128)(2,1)S(1)}, u32[]{:S(2)}, u32[]{:S(2)}) collective-permute-start(bf16[128,128]{1,0:T(8,128)(2,1)S(1)} %broadcast_select_fusion.2), channel_id=1, source_target_pairs={{0,128},{128,0},{16,144},{144,16},{32,160},{160,32},{48,176},{176,... | collective-permute-start | bytes 98312 | tf_op jit(solution)/shard_map/ppermute | solution.py:20
  165.2 16.5 %collective-permute-start.4 = (bf16[128,128]{1,0:T(8,128)(2,1)S(1)}, bf16[128,128]{1,0:T(8,128)(2,1)S(1)}, u32[]{:S(2)}, u32[]{:S(2)}) collective-permute-start(bf16[128,128]{1,0:T(8,128)(2,1)S(1)} %broadcast_select_fusion.8), channel_id=1, source_target_pairs={{0,256},{256,0},{16,272},{272,16},{32,288},{288,32},{48,304},{304,... | collective-permute-start | bytes 98312 | tf_op jit(solution)/shard_map/ppermute | solution.py:20
  177.2 24.6 %collective-permute-start.13 = (bf16[128,128]{1,0:T(8,128)(2,1)S(1)}, bf16[128,128]{1,0:T(8,128)(2,1)S(1)}, u32[]{:S(2)}, u32[]{:S(2)}) collective-permute-start(bf16[128,128]{1,0:T(8,128)(2,1)S(1)} %broadcast_select_fusion.3), channel_id=1, source_target_pairs={{0,256},{256,0},{16,272},{272,16},{32,288},{288,32},{48,304},{304,... | collective-permute-start | bytes 98312 | tf_op jit(solution)/shard_map/ppermute | solution.py:20
  420.6 21.7 %collective-permute-start.18 = (bf16[128,64]{0,1:T(8,128)(2,1)S(1)}, bf16[128,64]{0,1:T(8,128)(2,1)S(1)}, u32[]{:S(2)}, u32[]{:S(2)}) collective-permute-start(bf16[128,64]{0,1:T(8,128)(2,1)S(1)} %get-tuple-element.10), channel_id=1, source_target_pairs={{0,16},{16,0},{32,48},{48,32},{64,80},{80,64},{96,112},{112,96},{1... | collective-permute-start | bytes 49160 | tf_op jit(solution)/shard_map/ppermute | solution.py:20
  458.1 14.0 %collective-permute-start.21 = (bf16[128,64]{0,1:T(8,128)(2,1)S(1)}, bf16[128,64]{0,1:T(8,128)(2,1)S(1)}, u32[]{:S(2)}, u32[]{:S(2)}) collective-permute-start(bf16[128,64]{0,1:T(8,128)(2,1)S(1)} %broadcast_select_fusion.32), channel_id=1, source_target_pairs={{0,128},{128,0},{16,144},{144,16},{32,160},{160,32},{48,176},{176,... | collective-permute-start | bytes 49160 | tf_op jit(solution)/shard_map/ppermute | solution.py:20
  464.4 13.3 %collective-permute-start.25 = (bf16[128,64]{0,1:T(8,128)(2,1)S(1)}, bf16[128,64]{0,1:T(8,128)(2,1)S(1)}, u32[]{:S(2)}, u32[]{:S(2)}) collective-permute-start(bf16[128,64]{0,1:T(8,128)(2,1)S(1)} %broadcast_select_fusion.17), channel_id=1, source_target_pairs={{0,128},{128,0},{16,144},{144,16},{32,160},{160,32},{48,176},{176,... | collective-permute-start | bytes 49160 | tf_op jit(solution)/shard_map/ppermute | solution.py:20
  477.7 23.3 %collective-permute-start.26 = (bf16[128,64]{0,1:T(8,128)(2,1)S(1)}, bf16[128,64]{0,1:T(8,128)(2,1)S(1)}, u32[]{:S(2)}, u32[]{:S(2)}) collective-permute-start(bf16[128,64]{0,1:T(8,128)(2,1)S(1)} %broadcast_select_fusion.20), channel_id=1, source_target_pairs={{0,256},{256,0},{16,272},{272,16},{32,288},{288,32},{48,304},{304,... | collective-permute-start | bytes 49160 | tf_op jit(solution)/shard_map/ppermute | solution.py:20
  718.8 21.7 %collective-permute-start.27 = (bf16[128,64]{0,1:T(8,128)(2,1)S(1)}, bf16[128,64]{0,1:T(8,128)(2,1)S(1)}, u32[]{:S(2)}, u32[]{:S(2)}) collective-permute-start(bf16[128,64]{0,1:T(8,128)(2,1)S(1)} %get-tuple-element.6), channel_id=1, source_target_pairs={{0,16},{16,0},{32,48},{48,32},{64,80},{80,64},{96,112},{112,96},{1... | collective-permute-start | bytes 49160 | tf_op jit(solution)/shard_map/ppermute | solution.py:20
  751.0 13.3 %collective-permute-start.33 = (bf16[128,64]{0,1:T(8,128)(2,1)S(1)}, bf16[128,64]{0,1:T(8,128)(2,1)S(1)}, u32[]{:S(2)}, u32[]{:S(2)}) collective-permute-start(bf16[128,64]{0,1:T(8,128)(2,1)S(1)} %broadcast_select_fusion.13), channel_id=1, source_target_pairs={{0,64},{64,0},{16,80},{80,16},{32,96},{96,32},{48,112},{112,48},{1... | collective-permute-start | bytes 49160 | tf_op jit(solution)/shard_map/ppermute | solution.py:20
  756.3 14.0 %collective-permute-start.30 = (bf16[128,64]{0,1:T(8,128)(2,1)S(1)}, bf16[128,64]{0,1:T(8,128)(2,1)S(1)}, u32[]{:S(2)}, u32[]{:S(2)}) collective-permute-start(bf16[128,64]{0,1:T(8,128)(2,1)S(1)} %broadcast_select_fusion.31), channel_id=1, source_target_pairs={{0,128},{128,0},{16,144},{144,16},{32,160},{160,32},{48,176},{176,... | collective-permute-start | bytes 49160 | tf_op jit(solution)/shard_map/ppermute | solution.py:20
  777.6 23.6 %collective-permute-start.35 = (bf16[128,64]{0,1:T(8,128)(2,1)S(1)}, bf16[128,64]{0,1:T(8,128)(2,1)S(1)}, u32[]{:S(2)}, u32[]{:S(2)}) collective-permute-start(bf16[128,64]{0,1:T(8,128)(2,1)S(1)} %broadcast_select_fusion.19), channel_id=1, source_target_pairs={{0,256},{256,0},{16,272},{272,16},{32,288},{288,32},{48,304},{304,... | collective-permute-start | bytes 49160 | tf_op jit(solution)/shard_map/ppermute | solution.py:20
  (15 other events, 126.2 us)
where the time goes:
time: 922 us; the launch traced here: 920 us
  blocking collectives  729 us (79%)
  starting transfers between devices  162 us (18%)
  waiting for transfers between devices  12.4 us (1%)
    psum x3, blocking collectives, total_squares(): return lax.psum(jnp.sum(values * values, axis=0), ('blk', 'row'))  298 us
    psum x2, blocking collectives, local(): curvature = lax.psum(jnp.sum(direction * applied, axis=0), ('blk', 'row'))  197 us
    ppermute x36, starting transfers between devices, from_partner(): return lax.ppermute(block, axis, route)  162 us
    all_gather x6, blocking collectives, local(): lax.all_gather(fetch_results[apply_round_index], 'row', axis=0, tiled=True)  116 us
    all_gather x3, blocking collectives, local(): lax.all_gather(apply_rounded, 'row', axis=0, tiled=True)  56.4 us
    all_gather x2, blocking collectives, local(): lax.all_gather(group, 'row', axis=0, tiled=True)  37.5 us
    all_gather x1, blocking collectives, local(): block_features = lax.all_gather(features, 'row', axis=0, tiled=True)  23.8 us
  transfers between devices with their start and end apart: 36, of which 3 were waited for; matrix products, arithmetic and copies ran while one was open for 0% of the time, Pallas kernels for 0%

commit v1 on v0

v1 whole, which is shorter than its diff:
```python
import functools

import jax
import jax.numpy as jnp
import numpy as np
from jax import lax
from jax.experimental import pallas as pl
from jax.experimental.pallas import tpu as pltpu
from jax.sharding import PartitionSpec as P

MESH = pl.DeviceIdType.MESH
ITERS = 3
BLOCKS = 32
LAST = BLOCKS - 1
NEAR, ACROSS = 1, 16
NX, NYL, NZ = 4, 2, 16
CHIPS = 3 * NX * NYL
COLS = 32
LANES = 128


def hops(a, b):
    dz = abs(a % NZ - b % NZ)
    return min(dz, NZ - dz) + 2 * (a // NZ != b // NZ)


def placement(mask):
    groups, seen = [], set()
    for b in range(BLOCKS):
        if b not in seen:
            group = [b, b ^ LAST, b ^ mask, b ^ LAST ^ mask]
            seen.update(group)
            groups.append(group)
    offsets = [0, NEAR, ACROSS, NEAR ^ ACROSS]

    def cost(group, base, twist):
        lengths = [hops(b, base ^ o ^ twist) for b, o in zip(group, offsets)]
        return max(lengths), sum(lengths)

    bases = [p for p in range(BLOCKS) if not p & (NEAR | ACROSS)]
    best = [[min((cost(g, base, t), t) for t in offsets) for base in bases] for g in groups]
    state = {0: ((0, 0), [])}
    for g in range(len(groups)):
        following = {}
        for used, ((longest, total), chosen) in state.items():
            for i in range(len(bases)):
                if used >> i & 1:
                    continue
                (top, plus), twist = best[g][i]
                value = (max(longest, top), total + plus)
                key = used | 1 << i
                if key not in following or value < following[key][0]:
                    following[key] = (value, chosen + [(i, twist)])
        state = following
    _, chosen = state[(1 << len(bases)) - 1]
    place = [0] * BLOCKS
    for group, (i, twist) in zip(groups, chosen):
        for b, o in zip(group, offsets):
            place[b] = bases[i] ^ o ^ twist
    return place


def two_sum(a, b):
    s = a + b
    bb = s - a
    return s, (a - (s - bb)) + (b - bb)


def renorm(s, e):
    h = s + e
    return h, e - (h - s)


def pair_add(a, b):
    s, e = two_sum(a[0], b[0])
    return renorm(s, e + (a[1] + b[1]))


def split(a):
    c = 4097.0 * a
    h = c - (c - a)
    return h, a - h


def two_prod(a, b):
    p = a * b
    ah, al = split(a)
    bh, bl = split(b)
    return p, ((ah * bh - p) + ah * bl + al * bh) + al * bl


def pair_mul(a, b):
    p, e = two_prod(a[0], b[0])
    return renorm(p, e + (a[0] * b[1] + a[1] * b[0]))


def pair_tree(pair):
    n = pair[0].shape[0]
    while n > 1:
        n //= 2
        pair = pair_add(tuple(v[:n] for v in pair), tuple(v[n:] for v in pair))
    return pair


def squares(block):
    wide = block.astype(jnp.float32)
    return jnp.sum(wide * wide, axis=1, keepdims=True)


def kernel(
    x_ref, t_ref, sol_ref, res_ref,
    feats, tile, q_buf, r_buf, d_buf, w_buf, sol_buf, part, plane, line, back, own_rows, own_sq,
    f_send, f_recv, g_send, g_recv, t_send, t_recv, c_sem, q_send, q_recv, p_send, p_recv, z_send, z_recv, b_sem,
):
    blk, row = lax.axis_index("blk"), lax.axis_index("row")
    yh, z = blk // NZ, blk % NZ
    x, yl, c = row // 4, (row // 2) % 2, row % 2
    chip = x * NYL + yl
    other = {"row": row - c + (1 - c)}
    me = chip

    def coset_peer(k):
        side, rel = k // 8, k % 8
        px, pyl = (x + rel // 2) % NX, (yl + rel) % NYL
        near = jnp.where(side == 1, 1, 0)
        across = jnp.where(side == 2, 1, 0)
        pz = z + near * (1 - 2 * (z % 2))
        pyh = (yh + across) % 2
        return (pyh * NZ + pz, px * 4 + pyl * 2 + c), side * 8 + px * NYL + pyl, side * 8 + chip

    def plane_peer(k):
        y = (yh * 2 + yl + k) % 4
        px = (x + k // 4) % NX
        return ((y // 2) * NZ + z, px * 4 + (y % 2) * 2 + c), px * 4 + y

    def line_peer(k):
        pz = (z + k) % NZ
        return (yh * NZ + pz, row), pz

    plane_me = x * 4 + yh * 2 + yl

    barrier = pltpu.get_barrier_semaphore()

    def greet(peer):
        pl.semaphore_signal(barrier, inc=1, device_id=peer, device_id_type=MESH)

    greet((blk, row - c + (1 - c)))
    for first, last, peer in ((8, CHIPS, coset_peer), (1, 16, plane_peer), (1, 16, line_peer)):
        lax.fori_loop(first, last, lambda k, _, peer=peer: greet(peer(k)[0]) or 0, 0)
    pl.semaphore_wait(barrier, 1 + (CHIPS - 8) + 15 + 15)

    def f_copy(k):
        peer, here, there = coset_peer(k)
        return pltpu.make_async_remote_copy(
            x_ref, feats.at[there, c], f_send.at[k], f_recv.at[there], device_id=peer, device_id_type=MESH)

    def f_arrival(slot):
        return pltpu.make_async_remote_copy(
            x_ref, feats.at[slot, c], f_send.at[0], f_recv.at[slot], device_id=(blk, row), device_id_type=MESH)

    def g_copy(slot):
        return pltpu.make_async_remote_copy(
            feats.at[slot, c], feats.at[slot, c], g_send.at[slot], g_recv.at[slot],
            device_id=(blk, row - c + (1 - c)), device_id_type=MESH)

    def g_arrival(slot):
        return pltpu.make_async_remote_copy(
            feats.at[slot, 1 - c], feats.at[slot, 1 - c], g_send.at[slot], g_recv.at[slot],
            device_id=(blk, row - c + (1 - c)), device_id_type=MESH)

    flipped = t_ref[...].T
    back[0] = flipped[:COLS]
    back[1] = flipped[COLS:]
    d_buf[me, c] = back[c]
    t_swap = pltpu.make_async_remote_copy(
        back.at[1 - c], d_buf.at[me, c], c_sem.at[0], c_sem.at[1],
        device_id=(blk, row - c + (1 - c)), device_id_type=MESH)
    t_swap.start()

    feats[me, c] = x_ref[...]
    g_copy(me).start()

    def send_features(k, _):
        f_copy(k).start()
        return 0

    lax.fori_loop(1, CHIPS, send_features, 0)
    pltpu.make_async_remote_copy(
        back.at[1 - c], d_buf.at[me, 1 - c], c_sem.at[0], c_sem.at[1],
        device_id=(blk, row - c + (1 - c)), device_id_type=MESH).wait_recv()

    def t_copy(k, slot):
        peer, here, there = coset_peer(k)
        return pltpu.make_async_remote_copy(
            d_buf.at[me], d_buf.at[there if slot is None else slot], t_send.at[k],
            t_recv.at[there if slot is None else slot], device_id=peer, device_id_type=MESH)

    def send_targets(k, _):
        t_copy(k, None).start()
        return 0

    lax.fori_loop(1, CHIPS, send_targets, 0)

    g_arrival(me).wait_recv()
    for half in range(2):
        block = feats[me, half]
        own_rows[half * LANES:(half + 1) * LANES] = block
        own_sq[:, half * LANES:(half + 1) * LANES] = jnp.broadcast_to(squares(block), (LANES, LANES)).T[0:8]

    def fill(slot, half):
        block = feats[slot, half]
        g = lax.dot_general(block, own_rows[...], (((1,), (1,)), ((), ())), preferred_element_type=jnp.float32)
        e = (2.0 * g - squares(block) - own_sq[0:1, :]) * (1.0 / 128.0)
        at = pl.multiple_of((slot * 2 + half) * LANES, LANES)
        tile[pl.ds(at, LANES), :] = jnp.exp(e).astype(jnp.bfloat16)

    fill(me, 0)
    fill(me, 1)

    def direct(k, _):
        _, slot, _ = coset_peer(k)
        f_arrival(slot).wait_recv()
        g_copy(slot).start()
        fill(slot, c)
        return 0

    lax.fori_loop(1, CHIPS, direct, 0)

    def forwarded(k, _):
        _, slot, _ = coset_peer(k)
        g_arrival(slot).wait_recv()
        fill(slot, 1 - c)
        return 0

    lax.fori_loop(1, CHIPS, forwarded, 0)

    def first(k, _):
        _, slot, _ = coset_peer(k)

        @pl.when(k > 0)
        def _():
            t_copy(k, slot).wait_recv()

        for half in range(2):
            v = d_buf[slot, half]
            r_buf[slot, half] = v
            at = pl.multiple_of((slot * 2 + half) * LANES, LANES)
            w_buf[:, pl.ds(at, LANES)] = v.astype(jnp.bfloat16)
        return 0

    lax.fori_loop(0, CHIPS, first, 0)

    def q_copy(it, k, slot):
        peer, here, there = coset_peer(k)
        at = there if slot is None else slot
        return pltpu.make_async_remote_copy(
            q_buf.at[it, me], q_buf.at[it, at], q_send.at[it, k], q_recv.at[it, at],
            device_id=peer, device_id_type=MESH)

    def p_copy(it, k, slot):
        peer, _ = plane_peer(k)
        at = plane_me if slot is None else slot
        return pltpu.make_async_remote_copy(
            part.at[it, 0], plane.at[it, at], p_send.at[it, k], p_recv.at[it, at],
            device_id=peer, device_id_type=MESH)

    def z_copy(it, k, slot):
        peer, _ = line_peer(k)
        at = z if slot is None else slot
        return pltpu.make_async_remote_copy(
            part.at[it, 1], line.at[it, at], z_send.at[it, k], z_recv.at[it, at],
            device_id=peer, device_id_type=MESH)

    def exchange(it, stage, gathered, mine, copy, peer, pair):
        msg = jnp.concatenate(pair, axis=0)
        part[it, stage] = msg
        gathered[it, mine] = msg

        def send(k, _):
            copy(it, k, None).start()
            return 0

        lax.fori_loop(1, 16, send, 0)

    def collect(it, gathered, copy, peer):
        def wait(k, _):
            copy(it, k, peer(k)[1]).wait_recv()
            return 0

        lax.fori_loop(1, 16, wait, 0)
        return pair_tree((gathered[it, :, 0, :], gathered[it, :, 1, :]))

    for it in range(ITERS):
        own = jnp.dot(w_buf[:, :16 * LANES], tile[:16 * LANES], preferred_element_type=jnp.float32)
        others = jnp.dot(w_buf[:, 16 * LANES:], tile[16 * LANES:], preferred_element_type=jnp.float32)
        products = 2.0 * own + others
        slot_q = min(it, 1)
        sums = None
        fresh = []
        for half in range(2):
            d, r = d_buf[me, half], r_buf[me, half]
            q = d + products[:, half * LANES:(half + 1) * LANES]
            fresh.append(q)
            pairs = [two_prod(d, q), two_prod(r, q), two_prod(q, q), two_prod(r, r)]
            pair = tuple(jnp.concatenate([p[i] for p in pairs], axis=0) for i in range(2))
            sums = pair if sums is None else pair_add(sums, pair)
        if it < ITERS - 1:
            for half in range(2):
                q_buf[it, me, half] = fresh[half]
        pair = pair_tree(tuple(v.T for v in sums))
        exchange(it, 0, plane, plane_me, p_copy, plane_peer, pair)
        if it < ITERS - 1:
            def send_q(k, _):
                q_copy(it, k, None).start()
                return 0

            lax.fori_loop(1, CHIPS, send_q, 0)
        pair = collect(it, plane, p_copy, plane_peer)
        exchange(it, 1, line, z, z_copy, line_peer, pair)
        total = collect(it, line, z_copy, line_peer)

        def entry(i):
            return tuple(v[:, i * COLS:(i + 1) * COLS] for v in total)

        dq, rq, qq, rr = (entry(i) for i in range(4))
        step = rr[0] / dq[0]
        if it < ITERS - 1:
            zero = jnp.zeros_like(step)
            minus = pair_mul((-2.0 * step, zero), rq)
            plus = pair_mul(two_prod(step, step), qq)
            new = pair_add(pair_add(rr, minus), plus)
            ratio = new[0] / rr[0]
        else:
            ratio = jnp.zeros_like(step)
        scalars = jnp.concatenate([step, ratio, step, ratio], axis=1)
        scalars = jnp.broadcast_to(scalars, (LANES, LANES)).T
        s, beta = scalars[:COLS], scalars[COLS:2 * COLS]

        for half in range(2):
            gain = s * d_buf[me, half]
            sol_buf[0, half] = gain if it == 0 else sol_buf[0, half] + gain

        if it < ITERS - 1:
            def update(k, _):
                _, slot, _ = coset_peer(k)

                @pl.when(k > 0)
                def _():
                    q_copy(it, k, slot).wait_recv()

                for half in range(2):
                    r = r_buf[slot, half] - s * q_buf[it, slot, half]
                    d = r + beta * d_buf[slot, half]
                    r_buf[slot, half] = r
                    d_buf[slot, half] = d
                    at = pl.multiple_of((slot * 2 + half) * LANES, LANES)
                    w_buf[:, pl.ds(at, LANES)] = d.astype(jnp.bfloat16)
                return 0

            if it == 0:
                def sent(k, _):
                    t_copy(k, None).wait_send()
                    return 0

                lax.fori_loop(1, CHIPS, sent, 0)
            lax.fori_loop(0, CHIPS, update, 0)
        else:
            for half in range(2):
                sol_buf[1, half] = r_buf[me, half] - s * fresh[half]

    for i in range(2):
        pltpu.make_async_remote_copy(
            sol_buf.at[i, 1 - c], own_back(back, i, c), b_sem.at[0, i], b_sem.at[1, i],
            device_id=(blk, row - c + (1 - c)), device_id_type=MESH).start()
    for i, out in ((0, sol_ref), (1, res_ref)):
        back[2 + 2 * i + c] = sol_buf[i, c]
        pltpu.make_async_remote_copy(
            sol_buf.at[i, 1 - c], own_back(back, i, 1 - c), b_sem.at[0, i], b_sem.at[1, i],
            device_id=(blk, row - c + (1 - c)), device_id_type=MESH).wait()
        out[...] = jnp.concatenate([back[2 + 2 * i], back[3 + 2 * i]], axis=0).T

    t_swap.wait_send()
    g_copy(me).wait_send()

    def drain(k, _):
        f_copy(k).wait_send()
        _, slot, _ = coset_peer(k)
        g_copy(slot).wait_send()
        for it in range(ITERS - 1):
            q_copy(it, k, None).wait_send()
        return 0

    lax.fori_loop(1, CHIPS, drain, 0)

    def drain_sums(k, _):
        for it in range(ITERS):
            p_copy(it, k, None).wait_send()
            z_copy(it, k, None).wait_send()
        return 0

    lax.fori_loop(1, 16, drain_sums, 0)


def own_back(back, i, core):
    return back.at[2 + 2 * i + core]


def conjugate_gradients(features, targets):
    f32, bf16 = jnp.float32, jnp.bfloat16
    dma = pltpu.SemaphoreType.DMA
    return pl.pallas_call(
        kernel,
        out_shape=[jax.ShapeDtypeStruct(targets.shape, f32)] * 2,
        in_specs=[pl.BlockSpec(memory_space=pltpu.VMEM)] * 2,
        out_specs=[pl.BlockSpec(memory_space=pltpu.VMEM)] * 2,
        scratch_shapes=[
            pltpu.VMEM((CHIPS, 2, LANES, LANES), bf16),
            pltpu.VMEM((CHIPS * 2 * LANES, 2 * LANES), bf16),
            pltpu.VMEM((2, CHIPS, 2, COLS, LANES), f32),
            pltpu.VMEM((CHIPS, 2, COLS, LANES), f32),
            pltpu.VMEM((CHIPS, 2, COLS, LANES), f32),
            pltpu.VMEM((COLS, CHIPS * 2 * LANES), bf16),
            pltpu.VMEM((2, 2, COLS, LANES), f32),
            pltpu.VMEM((ITERS, 2, 2, LANES), f32),
            pltpu.VMEM((ITERS, 16, 2, LANES), f32),
            pltpu.VMEM((ITERS, 16, 2, LANES), f32),
            pltpu.VMEM((6, COLS, LANES), f32),
            pltpu.VMEM((2 * LANES, LANES), bf16),
            pltpu.VMEM((8, 2 * LANES), f32),
            dma((CHIPS,)), dma((CHIPS,)), dma((CHIPS,)), dma((CHIPS,)), dma((CHIPS,)), dma((CHIPS,)), dma((2,)),
            dma((2, CHIPS)), dma((2, CHIPS)),
            dma((ITERS, 16)), dma((ITERS, 16)), dma((ITERS, 16)), dma((ITERS, 16)),
            dma((2, 2)),
        ],
        compiler_params=pltpu.CompilerParams(
            collective_id=0, has_side_effects=True, vmem_limit_bytes=40 * 1024 * 1024
        ),
    )(features, targets)


def local(features, targets, round_masks):
    plans = [placement(mask) for mask in range(1, LAST)]
    which = jnp.clip(round_masks[0] + round_masks[1] - LAST - 1, 0, LAST - 2)

    def mover(route):
        return lambda a, b: (lax.ppermute(a, "blk", route), lax.ppermute(b, "blk", route))

    there = [mover([(b, p) for b, p in enumerate(plan)]) for plan in plans]
    back = [mover([(p, b) for b, p in enumerate(plan)]) for plan in plans]
    features, targets = lax.switch(which, there, features, targets)
    solution, residual = conjugate_gradients(features, targets)
    return lax.switch(which, back, solution, residual)


def solution(mesh):
    in_specs = (P(("blk", "row"), None), P(("blk", "row"), None), P())
    out_specs = (P(("blk", "row"), None), P(("blk", "row"), None))
    return jax.shard_map(local, mesh=mesh, in_specs=in_specs, out_specs=out_specs, check_vma=False)
```

time: 922 us -> 176 us (0.19)
  the two profiles are of different devices: /device:TPU:1 before, /device:TPU:49 now
where the time goes in v1:
time: 176 us
  Pallas kernels  102 us (58%)
  starting transfers between devices  48.8 us (28%)
  waiting for transfers between devices  19.2 us (11%)
  local copies, waits for them, and re-layouts  3.48 us (2%)
  between operations  1.95 us (1%)
    pallas_call x1, Pallas kernels, conjugate_gradients(): pl.pallas_call(kernel, out_shape=[jax.ShapeDtypeStruct(targets.shape, f32...  102 us
    ppermute x2, starting transfers between devices, mover(): lax.ppermute(a, 'blk', route)  25.3 us
    ppermute x2, starting transfers between devices, mover(): lax.ppermute(b, 'blk', route)  23.6 us
    ppermute x2, waiting for transfers between devices, mover(): lax.ppermute(a, 'blk', route)  9.94 us
    ppermute x2, waiting for transfers between devices, mover(): lax.ppermute(b, 'blk', route)  9.22 us
  transfers between devices with their start and end apart: 4, of which 3 were waited for; matrix products, arithmetic and copies ran while one was open for 1% of the time, Pallas kernels for 0%

profile of v1, /device:TPU:49, one launch (start us, length us, event | category | flops | bytes accessed | tf_op | source)
XLA Modules:
  0.0 175.5 jit_solution(4888335341046982509)
XLA Ops:
  0.6 0.0 copy-start
  0.6 0.6 copy-done
  1.3 0.6 fusion
  3.2 47.7 %conditional.2 = (bf16[128,128]{1,0:T(8,128)(2,1)}, f32[128,64]{1,0:T(8,128)}) conditional(s32[]{:T(128)} %bitcast, (bf16[128,128]{1,0:T(8,128)(2,1)}, f32[128,64]{0,1:T(8,128)}) %tuple.217, (bf16[128,128]{1,0:T(8,128)(2,1)}, f32[128,64]{0,1:T(8,128)}) %tuple.217, (bf16[128,128]{1,0:T(8,128)(2,1)}, ...), branch_computations={%region_0.1_spmd, %region_1.2_spmd, %region_2.3_spmd, %region_3.4_... | conditional | bytes 327776 | solution.py:450
  3.2 20.6 %collective-permute-start.48 = (bf16[128,128]{1,0:T(8,128)(2,1)}, bf16[128,128]{1,0:T(8,128)(2,1)}, u32[]{:S(2)}, u32[]{:S(2)}) collective-permute-start(bf16[128,128]{1,0:T(8,128)(2,1)} %get-tuple-element.288), channel_id=1, source_target_pairs={{0,48},{16,336},{32,0},{48,352},{64,272},{80,112},{96,288},{112,64... | collective-permute-start | bytes 98312 | tf_op jit(solution)/shard_map/cond/branch_24_fun/ppermute | solution.py:446
  23.9 0.8 copy.89
  24.7 19.0 %collective-permute-start.49 = (f32[128,64]{1,0:T(8,128)S(1)}, f32[128,64]{1,0:T(8,128)}, u32[]{:S(2)}, u32[]{:S(2)}) collective-permute-start(f32[128,64]{1,0:T(8,128)S(1)} %copy.89), channel_id=1, source_target_pairs={{0,48},{16,336},{32,0},{48,352},{64,272},{80,112},{96,288},{112,64... | collective-permute-start | bytes 98312 | tf_op jit(solution)/shard_map/cond/branch_24_fun/ppermute | solution.py:446
  43.7 0.0 collective-permute-done.48
  43.8 7.1 %collective-permute-done.49 = f32[128,64]{1,0:T(8,128)} collective-permute-done((f32[128,64]{1,0:T(8,128)S(1)}, f32[128,64]{1,0:T(8,128)}, u32[]{:S(2)}, u32[]{:S(2)}) %collective-permute-start.49) | collective-permute-done | bytes 32800 | tf_op jit(solution)/shard_map/cond/branch_24_fun/ppermute | solution.py:446
  50.9 101.8 %shard_map.110 = (f32[128,64]{1,0:T(8,128)S(1)}, f32[128,64]{1,0:T(8,128)S(1)}) custom-call(bf16[128,128]{1,0:T(8,128)(2,1)} %get-tuple-element.364.x_ref, f32[128,64]{1,0:T(8,128)} %get-tuple-element.365.t_ref), custom_call_target="tpu_custom_call" | custom-call | tf_op jit(solution)/shard_map/pallas_call | solution.py:411
  152.6 22.9 %conditional.3 = (f32[128,64]{0,1:T(8,128)}, f32[128,64]{0,1:T(8,128)}) conditional(s32[]{:T(128)} %bitcast, (f32[128,64]{1,0:T(8,128)S(1)}, f32[128,64]{1,0:T(8,128)S(1)}) %shard_map.110, (f32[128,64]{1,0:T(8,128)S(1)}, f32[128,64]{1,0:T(8,128)S(1)}) %shard_map.110, (f32[128,64]{1,0:T(8,128)S(1)}, ...), branch_computations={%region_30.31_spmd, %region_31.32_spmd, %region_32.33_spmd, %regio... | conditional | bytes 393312 | solution.py:452
  152.9 4.6 %collective-permute-start.108 = (f32[128,64]{1,0:T(8,128)S(1)}, f32[128,64]{1,0:T(8,128)S(1)}, u32[]{:S(2)}, u32[]{:S(2)}) collective-permute-start(f32[128,64]{1,0:T(8,128)S(1)} %get-tuple-element.348), channel_id=1, source_target_pairs={{48,0},{336,16},{0,32},{352,48},{272,64},{112,80},{288,96},{64,112... | collective-permute-start | bytes 98312 | tf_op jit(solution)/shard_map/cond/branch_24_fun/ppermute | solution.py:446
  157.5 4.6 %collective-permute-start.109 = (f32[128,64]{1,0:T(8,128)S(1)}, f32[128,64]{1,0:T(8,128)S(1)}, u32[]{:S(2)}, u32[]{:S(2)}) collective-permute-start(f32[128,64]{1,0:T(8,128)S(1)} %get-tuple-element.349), channel_id=1, source_target_pairs={{48,0},{336,16},{0,32},{352,48},{272,64},{112,80},{288,96},{64,112... | collective-permute-start | bytes 98312 | tf_op jit(solution)/shard_map/cond/branch_24_fun/ppermute | solution.py:446
  162.1 9.9 %collective-permute-done.108 = f32[128,64]{1,0:T(8,128)S(1)} collective-permute-done((f32[128,64]{1,0:T(8,128)S(1)}, f32[128,64]{1,0:T(8,128)S(1)}, u32[]{:S(2)}, u32[]{:S(2)}) %collective-permute-start.108) | collective-permute-done | bytes 32800 | tf_op jit(solution)/shard_map/cond/branch_24_fun/ppermute | solution.py:446
  172.0 0.7 copy.121
  172.7 2.1 %collective-permute-done.109 = f32[128,64]{1,0:T(8,128)S(1)} collective-permute-done((f32[128,64]{1,0:T(8,128)S(1)}, f32[128,64]{1,0:T(8,128)S(1)}, u32[]{:S(2)}, u32[]{:S(2)}) %collective-permute-start.109) | collective-permute-done | bytes 32800 | tf_op jit(solution)/shard_map/cond/branch_24_fun/ppermute | solution.py:446
  174.8 0.7 copy.151
Async XLA Ops:
  0.6 0.7 copy-start
  3.2 40.5 %collective-permute-start.48 = (bf16[128,128]{1,0:T(8,128)(2,1)}, bf16[128,128]{1,0:T(8,128)(2,1)}, u32[]{:S(2)}, u32[]{:S(2)}) collective-permute-start(bf16[128,128]{1,0:T(8,128)(2,1)} %get-tuple-element.288), channel_id=1, source_target_pairs={{0,48},{16,336},{32,0},{48,352},{64,272},{80,112},{96,288},{112,64... | collective-permute-start | bytes 98312 | tf_op jit(solution)/shard_map/cond/branch_24_fun/ppermute | solution.py:446
  24.7 26.1 %collective-permute-start.49 = (f32[128,64]{1,0:T(8,128)S(1)}, f32[128,64]{1,0:T(8,128)}, u32[]{:S(2)}, u32[]{:S(2)}) collective-permute-start(f32[128,64]{1,0:T(8,128)S(1)} %copy.89), channel_id=1, source_target_pairs={{0,48},{16,336},{32,0},{48,352},{64,272},{80,112},{96,288},{112,64... | collective-permute-start | bytes 98312 | tf_op jit(solution)/shard_map/cond/branch_24_fun/ppermute | solution.py:446
  152.9 19.1 %collective-permute-start.108 = (f32[128,64]{1,0:T(8,128)S(1)}, f32[128,64]{1,0:T(8,128)S(1)}, u32[]{:S(2)}, u32[]{:S(2)}) collective-permute-start(f32[128,64]{1,0:T(8,128)S(1)} %get-tuple-element.348), channel_id=1, source_target_pairs={{48,0},{336,16},{0,32},{352,48},{272,64},{112,80},{288,96},{64,112... | collective-permute-start | bytes 98312 | tf_op jit(solution)/shard_map/cond/branch_24_fun/ppermute | solution.py:446
  157.5 17.3 %collective-permute-start.109 = (f32[128,64]{1,0:T(8,128)S(1)}, f32[128,64]{1,0:T(8,128)S(1)}, u32[]{:S(2)}, u32[]{:S(2)}) collective-permute-start(f32[128,64]{1,0:T(8,128)S(1)} %get-tuple-element.349), channel_id=1, source_target_pairs={{48,0},{336,16},{0,32},{352,48},{272,64},{112,80},{288,96},{64,112... | collective-permute-start | bytes 98312 | tf_op jit(solution)/shard_map/cond/branch_24_fun/ppermute | solution.py:446
